TPU v7x, 32 devices: a whole 2x2x4 slice. The times are simulated.
32 devices in a mesh: chan: 8 (over z, x), win: 4 (over y, core).
Axes of the slice: x: 2, y: 2, z: 4, core: 2. Of those that a mesh axis runs over, the one named last changes fastest.
Arguments:
- spectra: bfloat16 [8, 128, 128, 2, 128], P('chan', None, 'win'), may hold values from -6 to 6
- counts: int32 [128, 8], P('win'), may hold values from 1 to 256
- partner: int32 [2, 8], replicated, may hold values from 0 to 7, as said below
Outputs:
- cross: bfloat16 [8, 2, 128, 128, 256], P('win', None, 'chan')
Inputs may be any that keep to these rules, and one draw needn't show every extreme that they name: Each row of partner is one cycle through all 8 blocks: a permutation with no block its own partner and no two blocks each other's partners.
All inputs are finite; a program needn't handle non-finite values.
Results may differ from a plain program's by a relative error of at most 0.015.
Values may be sent and summed in bfloat16 or wider, within the bound.
A program may use at most 128 MiB of HBM per device.

v0:
```python
import functools

import jax
import jax.numpy as jnp
from jax import lax
from jax.experimental import pallas as pl
from jax.experimental.pallas import tpu as pltpu
from jax.sharding import PartitionSpec as P

NSAMP = 256
EPS = 1e-06
LANES = 128
AHEAD = 2
MESH = pl.DeviceIdType.MESH


def flip(index, bits):
    out, place = index, 1
    while place <= bits:
        if bits & place:
            out = out + place * (1 - 2 * ((index // place) % 2))
        place *= 2
    return out


def kernel(cfg, x_ref, counts_ref, partner_ref, out_ref, *scratch):
    nchan, groups, sizes, chosen, rounds, windows, width = cfg
    (tall, raw, cts, wgt, inv, sem_as, sem_ar, sem_ys, sem_yr, sem_bs, sem_br,
     sem_cs, sem_cr, sem_ts, sem_tr) = scratch[:15]
    nsub, bins = len(sizes), sum(sizes)
    starts = [sum(sizes[:s]) for s in range(nsub)]
    held, send = scratch[15:15 + nsub], scratch[15 + nsub:]
    total_bins = nchan * bins
    me = lax.axis_index("chan")
    mine = lax.axis_index("win")
    across, beside = flip(mine, 2), flip(mine, 1)
    rows = 2 * windows

    barrier = pltpu.get_barrier_semaphore()
    for d in range(1, nchan):
        pl.semaphore_signal(barrier, 1, device_id={"chan": flip(me, d)}, device_id_type=MESH)
    for d in range(1, groups):
        pl.semaphore_signal(barrier, 1, device_id={"win": flip(mine, d)}, device_id_type=MESH)

    def to_bins(s, d, peer=None):
        peer = flip(me, d) if peer is None else peer
        return pltpu.make_async_remote_copy(
            src_ref=send[s].at[peer], dst_ref=held[s].at[me, mine],
            send_sem=sem_as.at[s, d], recv_sem=sem_ar.at[s, d],
            device_id={"chan": peer}, device_id_type=MESH)

    half, quarter = nchan // 2, nchan // 4
    inner = ((me // half) + (me // quarter)) % 2

    def send_next(s, turn):
        d = nchan - turn
        peer = flip(me, d)
        if d >= half:
            peer = peer + inner * quarter * (1 - 2 * ((peer // quarter) % 2))
            d = d + inner * quarter * (1 - 2 * ((d // quarter) % 2))
        to_bins(s, d, peer).start()

    def to_across(s, d):
        block = held[s].at[flip(me, d), mine]
        return pltpu.make_async_remote_copy(
            src_ref=block, dst_ref=block, send_sem=sem_ys.at[s, d], recv_sem=sem_yr.at[s, d],
            device_id={"win": across}, device_id_type=MESH)

    def to_beside(s, d):
        block = held[s].at[flip(me, d), mine]
        return pltpu.make_async_remote_copy(
            src_ref=block, dst_ref=block, send_sem=sem_bs.at[s, d], recv_sem=sem_br.at[s, d],
            device_id={"win": beside}, device_id_type=MESH)

    def relay(s, d):
        block = held[s].at[flip(me, d), across]
        return pltpu.make_async_remote_copy(
            src_ref=block, dst_ref=block, send_sem=sem_cs.at[s, d], recv_sem=sem_cr.at[s, d],
            device_id={"win": beside}, device_id_type=MESH)

    def tallies(d):
        return pltpu.make_async_remote_copy(
            src_ref=tall.at[mine], dst_ref=tall.at[mine],
            send_sem=sem_ts.at[d], recv_sem=sem_tr.at[d],
            device_id={"win": flip(mine, d)}, device_id_type=MESH)

    def add_power(f, acc):
        v = x_ref[f].astype(jnp.float32)
        return acc + v * v

    acc = lax.fori_loop(0, total_bins, add_power, jnp.zeros((rows, width), jnp.float32), unroll=4)
    raw[0] = acc
    power = (raw[0, pl.ds(0, windows, stride=2), :] + raw[0, pl.ds(1, windows, stride=2), :]) * (1.0 / total_bins)
    scale = lax.rsqrt(power + EPS)

    def whiten(s):
        def one(j, carry):
            for q in range(sizes[s]):
                raw[q] = x_ref[j * bins + starts[s] + q].astype(jnp.float32)
            for q in range(sizes[s]):
                for k in range(2):
                    part = raw[q, pl.ds(k, windows, stride=2), :] * scale
                    send[s][j, q, pl.ds(k * windows, windows), :] = part.astype(jnp.bfloat16)
            return carry

        lax.fori_loop(0, nchan, one, 0)
        held[s][me, mine] = send[s][me]

    tall[mine] = jnp.zeros(tall.shape[1:], jnp.float32)
    tall[mine, :, pl.ds(0, windows)] = counts_ref[...].astype(jnp.float32)

    whiten(0)
    pl.semaphore_wait(barrier, nchan - 1 + groups - 1)
    to_across(0, 0).start()
    to_beside(0, 0).start()
    for turn in range(1, nchan):
        send_next(0, turn)
    for d in range(1, groups):
        tallies(d).start()
    for s in range(1, AHEAD):
        whiten(s)
        for turn in range(1, nchan):
            send_next(s, turn)

    def weights():
        for d in range(1, groups):
            tallies(d).wait_recv()
        whole = tall[0]
        for g in range(1, groups):
            whole = whole + pltpu.roll(tall[g], g * windows, 1)
        cts[...] = whole
        first = mine * chosen

        def one(n, carry):
            own = cts[pl.ds(first + n, 1), :]
            for r in range(rounds):
                row = jnp.minimum(own, cts[pl.ds(partner_ref[r, first + n], 1), :]) * (1.0 / NSAMP)
                wgt[n, r] = jnp.broadcast_to(row, (LANES, LANES)).T.astype(jnp.bfloat16)
                norm = lax.rsqrt(jnp.sum(row * row, axis=1, keepdims=True))
                inv[n, r] = jnp.broadcast_to(norm, (8, width))
            return carry

        lax.fori_loop(0, chosen, one, 0)

    def planes(s, block, q):
        return [
            jnp.concatenate(
                [held[s][block, g, q, pl.ds(k * windows, windows), :] for g in range(groups)], axis=0)
            for k in range(2)
        ]

    def unit(s, u):
        n, q = u // sizes[s], u % sizes[s]
        a = mine * chosen + n
        re, im = planes(s, a, q)
        re, im = re.T, im.T
        lhs = jnp.concatenate(
            [jnp.concatenate([re, im], axis=1), jnp.concatenate([im, -re], axis=1)], axis=0)
        mates = []
        for r in range(rounds):
            w = wgt[n, r]
            mre, mim = planes(s, partner_ref[r, a], q)
            mates.append(jnp.concatenate([mre * w, mim * w], axis=0))
        rhs = jnp.concatenate(mates, axis=1)
        res = jnp.dot(lhs, rhs, preferred_element_type=jnp.float32)
        for r in range(rounds):
            norm = inv[n, r, pl.ds(0, 1), :]
            for k in range(2):
                tile = res[k * width:(k + 1) * width, r * width:(r + 1) * width] * norm
                out_ref[n, r, starts[s] + q, :, pl.ds(k * width, width)] = tile.astype(jnp.bfloat16)

    def compute(s, low, high):
        lax.fori_loop(low, high, lambda u, carry: (unit(s, u), carry)[1], 0, unroll=2 if (high - low) % 2 == 0 else 1)

    def settle(s):
        for d in range(nchan):
            to_beside(s, d).wait_recv()
            relay(s, d).wait_recv()

    def pass_on(step):
        s, d = step // nchan, step % nchan
        to_across(s, d).wait_recv()
        relay(s, d).start()

    lag = nchan // 2
    late = 5 * nchan // 8
    for s in range(nsub):
        units = chosen * sizes[s - 1]
        for d in range(nchan):
            step = s * nchan + d
            if d:
                to_bins(s, d).wait_recv()
            if step:
                to_across(s, d).start()
                to_beside(s, d).start()
            if d == 0 and s + AHEAD < nsub:
                whiten(s + AHEAD)
            if d and s + AHEAD < nsub:
                send_next(s + AHEAD, d)
            if step >= lag:
                pass_on(step - lag)
            if step == nchan - 1:
                weights()
            if s and d >= late:
                if d == late:
                    settle(s - 1)
                i = d - late
                compute(s - 1, i * units // (nchan - late), (i + 1) * units // (nchan - late))
    for step in range(nsub * nchan - lag, nsub * nchan):
        pass_on(step)
    settle(nsub - 1)
    compute(nsub - 1, 0, chosen * sizes[-1])

    for d in range(1, groups):
        tallies(d).wait_send()
    for s in range(nsub):
        for d in range(nchan):
            if d:
                to_bins(s, d).wait_send()
            to_across(s, d).wait_send()
            to_beside(s, d).wait_send()
            relay(s, d).wait_send()


def per_device(nchan, groups, spectra, counts, partner):
    _, total_bins, windows, parts, width = spectra.shape
    rounds, nblocks = partner.shape
    bins = total_bins // nchan
    chosen = nblocks // groups
    sizes = (bins // 4,) * 3 + (bins // 8,) * 2 if bins % 8 == 0 else (1,) * bins
    nsub = len(sizes)
    cfg = (nchan, groups, sizes, chosen, rounds, windows, width)
    x = spectra.reshape(total_bins, windows * parts, width)
    dma = pltpu.SemaphoreType.DMA
    flops = 2 * chosen * rounds * bins * width * (2 * width) * (2 * groups * windows)
    return pl.pallas_call(
        functools.partial(kernel, cfg),
        out_shape=jax.ShapeDtypeStruct((chosen, rounds, bins, width, 2 * width), jnp.bfloat16),
        in_specs=[
            pl.BlockSpec(memory_space=pltpu.VMEM),
            pl.BlockSpec(memory_space=pltpu.VMEM),
            pl.BlockSpec(memory_space=pltpu.SMEM),
        ],
        out_specs=pl.BlockSpec(memory_space=pltpu.VMEM),
        scratch_shapes=[
            pltpu.VMEM((groups, nblocks, LANES), jnp.float32),
            pltpu.VMEM((max(sizes), 2 * windows, width), jnp.float32),
            pltpu.VMEM((nblocks, LANES), jnp.float32),
            pltpu.VMEM((chosen, rounds, groups * windows, width), jnp.bfloat16),
            pltpu.VMEM((chosen, rounds, 8, width), jnp.float32),
        ]
        + [dma((nsub, nchan))] * 8
        + [dma((groups,))] * 2
        + [pltpu.VMEM((nblocks, groups, size, 2 * windows, width), jnp.bfloat16) for size in sizes]
        + [pltpu.VMEM((nchan, size, 2 * windows, width), jnp.bfloat16) for size in sizes],
        compiler_params=pltpu.CompilerParams(
            collective_id=0, has_side_effects=True, vmem_limit_bytes=40 * 1024 * 1024),
        cost_estimate=pl.CostEstimate(flops=flops, bytes_accessed=8 << 20, transcendentals=0),
    )(x, counts.T, partner)


def solution(mesh):
    sizes = dict(mesh.shape)
    placed = (P("chan", None, "win", None, None), P("win", None), P())
    return jax.shard_map(
        functools.partial(per_device, sizes["chan"], sizes["win"]),
        mesh=mesh,
        in_specs=placed,
        out_specs=P("win", None, "chan", None, None),
        check_vma=False,
    )
```

profile of v0, /device:TPU:1, one launch (start us, length us, event | category | flops | bytes accessed | tf_op | source)
XLA Modules:
  0.0 74.7 jit_solution(5507513702337416872)
XLA Ops:
  0.0 0.0 copy-start
  0.0 1.6 %copy-done = bf16[1,128,32,2,128]{4,3,2,1,0:T(2,128)(2,1)S(1)} copy-done((bf16[1,128,32,2,128]{4,3,2,1,0:T(2,128)(2,1)S(1)}, bf16[1,128,32,2,128]{4,3,2,1,0:T(2,128)(2,1)}, u32[]{:S(2)}) %copy-start) | copy-done | bytes 2097176
  1.6 0.0 copy-start.1
  1.6 0.7 copy-done.1
  2.3 0.0 copy-start.2
  2.3 0.7 copy-done.2
  3.0 69.8 %shard_map.37 = bf16[2,2,16,128,256]{4,3,2,1,0:T(8,128)(2,1)S(1)} custom-call(bf16[128,64,128]{2,1,0:T(8,128)(2,1)S(1)} %bitcast.2, s32[8,32]{1,0:T(8,128)S(1)} %bitcast.3, s32[2,8]{1,0:T(2,128)S(1)} %copy-done.2), custom_call_target="tpu_custom_call" | custom-call | flops 1073741824 | bytes 8388608 | tf_op jit(solution)/shard_map/pallas_call | solution.py:236
  72.7 2.0 %copy.5 = bf16[2,2,16,128,256]{4,3,2,1,0:T(8,128)(2,1)} copy(bf16[2,2,16,128,256]{4,3,2,1,0:T(8,128)(2,1)S(1)} %shard_map.37) | data formatting | bytes 8388608
Async XLA Ops:
  0.0 1.6 %copy-start = (bf16[1,128,32,2,128]{4,3,2,1,0:T(2,128)(2,1)S(1)}, bf16[1,128,32,2,128]{4,3,2,1,0:T(2,128)(2,1)}, u32[]{:S(2)}) copy-start(bf16[1,128,32,2,128]{4,3,2,1,0:T(2,128)(2,1)} %param.3) | copy-start | bytes 6291460
  1.6 0.7 copy-start.1
  2.3 0.7 copy-start.2
where the time goes:
time: 75.8 us; the launch traced here: 74.7 us
  Pallas kernels  69.8 us (92%)
  local copies, waits for them, and re-layouts  4.97 us (7%)
    pallas_call x1, Pallas kernels, per_device(): pl.pallas_call(functools.partial(kernel, cfg), out_shape=jax.ShapeDtypeSt...  69.8 us
    unnamed x7, local copies, waits for them, and re-layouts  4.97 us

commit v1 on v0

--- a/solution.py
+++ b/solution.py
@@ -52,13 +52,18 @@
     half, quarter = nchan // 2, nchan // 4
     inner = ((me // half) + (me // quarter)) % 2
 
-    def send_next(s, turn):
-        d = nchan - turn
+    def send_one(s, d):
         peer = flip(me, d)
         if d >= half:
             peer = peer + inner * quarter * (1 - 2 * ((peer // quarter) % 2))
             d = d + inner * quarter * (1 - 2 * ((d // quarter) % 2))
         to_bins(s, d, peer).start()
+
+    near, far = range(1, half), range(nchan - 1, half - 1, -1)
+
+    def send_all(s):
+        for d in (*near, *far):
+            send_one(s, d)
 
     def to_across(s, d):
         block = held[s].at[flip(me, d), mine]
@@ -113,14 +118,12 @@
     pl.semaphore_wait(barrier, nchan - 1 + groups - 1)
     to_across(0, 0).start()
     to_beside(0, 0).start()
-    for turn in range(1, nchan):
-        send_next(0, turn)
+    send_all(0)
     for d in range(1, groups):
         tallies(d).start()
-    for s in range(1, AHEAD):
+    for s in range(1, min(AHEAD, nsub)):
         whiten(s)
-        for turn in range(1, nchan):
-            send_next(s, turn)
+        send_all(s)
 
     def weights():
         for d in range(1, groups):
@@ -177,39 +180,50 @@
             to_beside(s, d).wait_recv()
             relay(s, d).wait_recv()
 
-    def pass_on(step):
-        s, d = step // nchan, step % nchan
+    order = [(0, d) for d in range(half)]
+    for s in range(nsub):
+        if s + 1 < nsub:
+            order += [(s + 1, d) for d in range(half)]
+        order += [(s, d) for d in range(half, nchan)]
+
+    def pass_on(s, d):
         to_across(s, d).wait_recv()
         relay(s, d).start()
 
-    lag = nchan // 2
-    late = 5 * nchan // 8
-    for s in range(nsub):
-        units = chosen * sizes[s - 1]
-        for d in range(nchan):
-            step = s * nchan + d
-            if d:
-                to_bins(s, d).wait_recv()
-            if step:
-                to_across(s, d).start()
-                to_beside(s, d).start()
-            if d == 0 and s + AHEAD < nsub:
-                whiten(s + AHEAD)
-            if d and s + AHEAD < nsub:
-                send_next(s + AHEAD, d)
-            if step >= lag:
-                pass_on(step - lag)
-            if step == nchan - 1:
-                weights()
-            if s and d >= late:
-                if d == late:
-                    settle(s - 1)
-                i = d - late
-                compute(s - 1, i * units // (nchan - late), (i + 1) * units // (nchan - late))
-    for step in range(nsub * nchan - lag, nsub * nchan):
-        pass_on(step)
+    def share(s, i, count):
+        units = chosen * sizes[s]
+        compute(s, i * units // count, (i + 1) * units // count)
+
+    lag = half
+    skip = half // 4
+    for step, (s, d) in enumerate(order):
+        if d:
+            to_bins(s, d).wait_recv()
+        if step:
+            to_across(s, d).start()
+            to_beside(s, d).start()
+        if d == 0 and 0 < s < nsub - 1:
+            whiten(s + 1)
+            for e in near:
+                send_one(s + 1, e)
+        if d >= half and s + AHEAD < nsub:
+            send_one(s + AHEAD, nchan - 1 - (d - half))
+        if step >= lag:
+            pass_on(*order[step - lag])
+        if step == nchan - 1:
+            weights()
+        if 0 < s < nsub - 1 and d >= half + skip:
+            if d == half + skip:
+                settle(s - 1)
+            share(s - 1, d - half - skip, half - skip)
+    for i, (s, d) in enumerate(order[-lag:]):
+        pass_on(s, d)
+        if nsub > 1:
+            if i == 0:
+                settle(nsub - 2)
+            share(nsub - 2, i, lag)
     settle(nsub - 1)
-    compute(nsub - 1, 0, chosen * sizes[-1])
+    share(nsub - 1, 0, 1)
 
     for d in range(1, groups):
         tallies(d).wait_send()

time: 75.8 us -> 69.2 us (0.913); the launches traced: 74.7 us -> 69 us
  Pallas kernels: 69.8 us -> 64.1 us
    pallas_call x1, Pallas kernels: 69.8 us -> 64.1 us  [per_device(): pl.pallas_call(functools.partial(kernel, cfg), out_shape=jax.ShapeDtypeSt...]
where the time goes in v1:
time: 69.2 us; the launch traced here: 69 us
  Pallas kernels  64.1 us (93%)
  local copies, waits for them, and re-layouts  4.97 us (7%)
    pallas_call x1, Pallas kernels, per_device(): pl.pallas_call(functools.partial(kernel, cfg), out_shape=jax.ShapeDtypeSt...  64.1 us
    unnamed x7, local copies, waits for them, and re-layouts  4.97 us

profile of v1, /device:TPU:1, one launch (start us, length us, event | category | flops | bytes accessed | tf_op | source)
XLA Modules:
  0.0 69.0 jit_solution(9088001929337476527)
XLA Ops:
  0.0 0.0 copy-start
  0.0 1.6 %copy-done = bf16[1,128,32,2,128]{4,3,2,1,0:T(2,128)(2,1)S(1)} copy-done((bf16[1,128,32,2,128]{4,3,2,1,0:T(2,128)(2,1)S(1)}, bf16[1,128,32,2,128]{4,3,2,1,0:T(2,128)(2,1)}, u32[]{:S(2)}) %copy-start) | copy-done | bytes 2097176
  1.6 0.0 copy-start.1
  1.6 0.7 copy-done.1
  2.3 0.0 copy-start.2
  2.3 0.7 copy-done.2
  3.0 64.1 %shard_map.37 = bf16[2,2,16,128,256]{4,3,2,1,0:T(8,128)(2,1)S(1)} custom-call(bf16[128,64,128]{2,1,0:T(8,128)(2,1)S(1)} %bitcast.2, s32[8,32]{1,0:T(8,128)S(1)} %bitcast.3, s32[2,8]{1,0:T(2,128)S(1)} %copy-done.2), custom_call_target="tpu_custom_call" | custom-call | flops 1073741824 | bytes 8388608 | tf_op jit(solution)/shard_map/pallas_call | solution.py:250
  67.0 2.0 %copy.5 = bf16[2,2,16,128,256]{4,3,2,1,0:T(8,128)(2,1)} copy(bf16[2,2,16,128,256]{4,3,2,1,0:T(8,128)(2,1)S(1)} %shard_map.37) | data formatting | bytes 8388608
Async XLA Ops:
  0.0 1.6 %copy-start = (bf16[1,128,32,2,128]{4,3,2,1,0:T(2,128)(2,1)S(1)}, bf16[1,128,32,2,128]{4,3,2,1,0:T(2,128)(2,1)}, u32[]{:S(2)}) copy-start(bf16[1,128,32,2,128]{4,3,2,1,0:T(2,128)(2,1)} %param.3) | copy-start | bytes 6291460
  1.6 0.7 copy-start.1
  2.3 0.7 copy-start.2

commit v2 on v1

--- a/solution.py
+++ b/solution.py
@@ -10,7 +10,6 @@
 NSAMP = 256
 EPS = 1e-06
 LANES = 128
-AHEAD = 2
 MESH = pl.DeviceIdType.MESH
 
 
@@ -61,8 +60,8 @@
 
     near, far = range(1, half), range(nchan - 1, half - 1, -1)
 
-    def send_all(s):
-        for d in (*near, *far):
+    def send_part(s, part):
+        for d in part:
             send_one(s, d)
 
     def to_across(s, d):
@@ -118,12 +117,13 @@
     pl.semaphore_wait(barrier, nchan - 1 + groups - 1)
     to_across(0, 0).start()
     to_beside(0, 0).start()
-    send_all(0)
+    send_part(0, near)
     for d in range(1, groups):
         tallies(d).start()
-    for s in range(1, min(AHEAD, nsub)):
-        whiten(s)
-        send_all(s)
+    if nsub > 1:
+        whiten(1)
+        send_part(1, near)
+    send_part(0, far)
 
     def weights():
         for d in range(1, groups):
@@ -202,12 +202,17 @@
         if step:
             to_across(s, d).start()
             to_beside(s, d).start()
-        if d == 0 and 0 < s < nsub - 1:
-            whiten(s + 1)
-            for e in near:
-                send_one(s + 1, e)
-        if d >= half and s + AHEAD < nsub:
-            send_one(s + AHEAD, nchan - 1 - (d - half))
+        if step == 1:
+            if nsub > 2:
+                whiten(2)
+                send_part(2, near)
+            if nsub > 1:
+                send_part(1, far)
+        if d == half and s + 3 < nsub:
+            whiten(s + 3)
+            send_part(s + 3, near)
+        if d >= half and s + 2 < nsub:
+            send_one(s + 2, nchan - 1 - (d - half))
         if step >= lag:
             pass_on(*order[step - lag])
         if step == nchan - 1:

time: 69.2 us -> 68.6 us (level)
  Pallas kernels: 64.1 us -> 63.4 us
where the time goes in v2:
time: 68.6 us; the launch traced here: 68.4 us
  Pallas kernels  63.4 us (92%)
  local copies, waits for them, and re-layouts  4.97 us (7%)
    pallas_call x1, Pallas kernels, per_device(): pl.pallas_call(functools.partial(kernel, cfg), out_shape=jax.ShapeDtypeSt...  63.4 us
    unnamed x7, local copies, waits for them, and re-layouts  4.97 us

profile of v2, /device:TPU:1, one launch (start us, length us, event | category | flops | bytes accessed | tf_op | source)
XLA Modules:
  0.0 68.4 jit_solution(17552322055823519127)
XLA Ops:
  0.0 0.0 copy-start
  0.0 1.6 %copy-done = bf16[1,128,32,2,128]{4,3,2,1,0:T(2,128)(2,1)S(1)} copy-done((bf16[1,128,32,2,128]{4,3,2,1,0:T(2,128)(2,1)S(1)}, bf16[1,128,32,2,128]{4,3,2,1,0:T(2,128)(2,1)}, u32[]{:S(2)}) %copy-start) | copy-done | bytes 2097176
  1.6 0.0 copy-start.1
  1.6 0.7 %copy-done.1 = s32[32,8]{0,1:T(8,128)S(1)} copy-done((s32[32,8]{0,1:T(8,128)S(1)}, s32[32,8]{0,1:T(8,128)}, u32[]{:S(2)}) %copy-start.1) | copy-done | bytes 1048
  2.3 0.0 copy-start.2
  2.3 0.7 copy-done.2
  3.0 63.4 %shard_map.37 = bf16[2,2,16,128,256]{4,3,2,1,0:T(8,128)(2,1)S(1)} custom-call(bf16[128,64,128]{2,1,0:T(8,128)(2,1)S(1)} %bitcast.2, s32[8,32]{1,0:T(8,128)S(1)} %bitcast.3, s32[2,8]{1,0:T(2,128)S(1)} %copy-done.2), custom_call_target="tpu_custom_call" | custom-call | flops 1073741824 | bytes 8388608 | tf_op jit(solution)/shard_map/pallas_call | solution.py:255
  66.4 2.0 %copy.5 = bf16[2,2,16,128,256]{4,3,2,1,0:T(8,128)(2,1)} copy(bf16[2,2,16,128,256]{4,3,2,1,0:T(8,128)(2,1)S(1)} %shard_map.37) | data formatting | bytes 8388608
Async XLA Ops:
  0.0 1.6 %copy-start = (bf16[1,128,32,2,128]{4,3,2,1,0:T(2,128)(2,1)S(1)}, bf16[1,128,32,2,128]{4,3,2,1,0:T(2,128)(2,1)}, u32[]{:S(2)}) copy-start(bf16[1,128,32,2,128]{4,3,2,1,0:T(2,128)(2,1)} %param.3) | copy-start | bytes 6291460
  1.6 0.7 %copy-start.1 = (s32[32,8]{0,1:T(8,128)S(1)}, s32[32,8]{0,1:T(8,128)}, u32[]{:S(2)}) copy-start(s32[32,8]{0,1:T(8,128)} %param.4) | copy-start | bytes 3076
  2.3 0.7 copy-start.2

commit v3 on v2

--- a/solution.py
+++ b/solution.py
@@ -246,7 +246,8 @@
     rounds, nblocks = partner.shape
     bins = total_bins // nchan
     chosen = nblocks // groups
-    sizes = (bins // 4,) * 3 + (bins // 8,) * 2 if bins % 8 == 0 else (1,) * bins
+    unit = bins // 16
+    sizes = (4 * unit, 4 * unit, 4 * unit, 3 * unit, unit) if bins % 16 == 0 else (1,) * bins
     nsub = len(sizes)
     cfg = (nchan, groups, sizes, chosen, rounds, windows, width)
     x = spectra.reshape(total_bins, windows * parts, width)

time: 68.6 us -> 69.7 us (1.016)
  Pallas kernels: 63.4 us -> 64.5 us
    pallas_call x1, Pallas kernels: 63.4 us -> 64.5 us  [per_device(): pl.pallas_call(functools.partial(kernel, cfg), out_shape=jax.ShapeDtypeSt...]
where the time goes in v3:
time: 69.7 us; the launch traced here: 69.5 us
  Pallas kernels  64.5 us (93%)
  local copies, waits for them, and re-layouts  4.97 us (7%)
    pallas_call x1, Pallas kernels, per_device(): pl.pallas_call(functools.partial(kernel, cfg), out_shape=jax.ShapeDtypeSt...  64.5 us
    unnamed x7, local copies, waits for them, and re-layouts  4.97 us

profile of v3, /device:TPU:1, one launch (start us, length us, event | category | flops | bytes accessed | tf_op | source)
XLA Modules:
  0.0 69.5 jit_solution(3921445420163826572)
XLA Ops:
  0.0 0.0 copy-start
  0.0 1.6 %copy-done = bf16[1,128,32,2,128]{4,3,2,1,0:T(2,128)(2,1)S(1)} copy-done((bf16[1,128,32,2,128]{4,3,2,1,0:T(2,128)(2,1)S(1)}, bf16[1,128,32,2,128]{4,3,2,1,0:T(2,128)(2,1)}, u32[]{:S(2)}) %copy-start) | copy-done | bytes 2097176
  1.6 0.0 copy-start.1
  1.6 0.7 copy-done.1
  2.3 0.0 copy-start.2
  2.3 0.7 copy-done.2
  3.0 64.5 %shard_map.37 = bf16[2,2,16,128,256]{4,3,2,1,0:T(8,128)(2,1)S(1)} custom-call(bf16[128,64,128]{2,1,0:T(8,128)(2,1)S(1)} %bitcast.2, s32[8,32]{1,0:T(8,128)S(1)} %bitcast.3, s32[2,8]{1,0:T(2,128)S(1)} %copy-done.2), custom_call_target="tpu_custom_call" | custom-call | flops 1073741824 | bytes 8388608 | tf_op jit(solution)/shard_map/pallas_call | solution.py:256
  67.5 2.0 %copy.5 = bf16[2,2,16,128,256]{4,3,2,1,0:T(8,128)(2,1)} copy(bf16[2,2,16,128,256]{4,3,2,1,0:T(8,128)(2,1)S(1)} %shard_map.37) | data formatting | bytes 8388608
Async XLA Ops:
  0.0 1.6 %copy-start = (bf16[1,128,32,2,128]{4,3,2,1,0:T(2,128)(2,1)S(1)}, bf16[1,128,32,2,128]{4,3,2,1,0:T(2,128)(2,1)}, u32[]{:S(2)}) copy-start(bf16[1,128,32,2,128]{4,3,2,1,0:T(2,128)(2,1)} %param.3) | copy-start | bytes 6291460
  1.6 0.7 copy-start.1
  2.3 0.7 copy-start.2

commit v4 on v2

--- a/solution.py
+++ b/solution.py
@@ -246,7 +246,8 @@
     rounds, nblocks = partner.shape
     bins = total_bins // nchan
     chosen = nblocks // groups
-    sizes = (bins // 4,) * 3 + (bins // 8,) * 2 if bins % 8 == 0 else (1,) * bins
+    unit = bins // 8
+    sizes = (unit, 2 * unit, 2 * unit, unit, unit, unit) if bins % 8 == 0 else (1,) * bins
     nsub = len(sizes)
     cfg = (nchan, groups, sizes, chosen, rounds, windows, width)
     x = spectra.reshape(total_bins, windows * parts, width)

time: 68.6 us -> 69.6 us (1.015)
  Pallas kernels: 63.4 us -> 64.5 us
    pallas_call x1, Pallas kernels: 63.4 us -> 64.5 us  [per_device(): pl.pallas_call(functools.partial(kernel, cfg), out_shape=jax.ShapeDtypeSt...]
where the time goes in v4:
time: 69.6 us; the launch traced here: 69.5 us
  Pallas kernels  64.5 us (93%)
  local copies, waits for them, and re-layouts  4.97 us (7%)
    pallas_call x1, Pallas kernels, per_device(): pl.pallas_call(functools.partial(kernel, cfg), out_shape=jax.ShapeDtypeSt...  64.5 us
    unnamed x7, local copies, waits for them, and re-layouts  4.97 us

profile of v4, /device:TPU:1, one launch (start us, length us, event | category | flops | bytes accessed | tf_op | source)
XLA Modules:
  0.0 69.5 jit_solution(13639805277495671431)
XLA Ops:
  0.0 0.0 copy-start
  0.0 1.6 %copy-done = bf16[1,128,32,2,128]{4,3,2,1,0:T(2,128)(2,1)S(1)} copy-done((bf16[1,128,32,2,128]{4,3,2,1,0:T(2,128)(2,1)S(1)}, bf16[1,128,32,2,128]{4,3,2,1,0:T(2,128)(2,1)}, u32[]{:S(2)}) %copy-start) | copy-done | bytes 2097176
  1.6 0.0 copy-start.1
  1.6 0.7 copy-done.1
  2.3 0.0 copy-start.2
  2.3 0.7 copy-done.2
  3.0 64.5 %shard_map.37 = bf16[2,2,16,128,256]{4,3,2,1,0:T(8,128)(2,1)S(1)} custom-call(bf16[128,64,128]{2,1,0:T(8,128)(2,1)S(1)} %bitcast.2, s32[8,32]{1,0:T(8,128)S(1)} %bitcast.3, s32[2,8]{1,0:T(2,128)S(1)} %copy-done.2), custom_call_target="tpu_custom_call" | custom-call | flops 1073741824 | bytes 8388608 | tf_op jit(solution)/shard_map/pallas_call | solution.py:256
  67.4 2.0 %copy.5 = bf16[2,2,16,128,256]{4,3,2,1,0:T(8,128)(2,1)} copy(bf16[2,2,16,128,256]{4,3,2,1,0:T(8,128)(2,1)S(1)} %shard_map.37) | data formatting | bytes 8388608
Async XLA Ops:
  0.0 1.6 %copy-start = (bf16[1,128,32,2,128]{4,3,2,1,0:T(2,128)(2,1)S(1)}, bf16[1,128,32,2,128]{4,3,2,1,0:T(2,128)(2,1)}, u32[]{:S(2)}) copy-start(bf16[1,128,32,2,128]{4,3,2,1,0:T(2,128)(2,1)} %param.3) | copy-start | bytes 6291460
  1.6 0.7 copy-start.1
  2.3 0.7 copy-start.2
